TPU v7x, 512 devices: a whole 4x8x8 slice. The times are simulated.
512 devices in a mesh: feat: 32 (over y, x), samp: 8 (over z), rep: 2 (over core).
Axes of the slice: x: 4, y: 8, z: 8, core: 2. Of those that a mesh axis runs over, the one named last changes fastest.
Arguments:
- tiles: bfloat16 [32, 16, 32, 128, 256], P('feat', ('samp', 'rep')), may hold values from -0.25 to 0.25
- tile_block: int32 [32, 16, 32], P('feat', ('samp', 'rep')), may hold values from -1 to 63, as said below
- tile_row: int32 [32, 16, 32], P('feat', ('samp', 'rep')), may hold values from 0 to 31
- labels: int32 [65536], P(('samp', 'rep')), may hold values 0 or 1
- weights: float32 [524288], P('feat')
- hess_inv: float32 [2048, 256, 256], P(('feat', 'samp', 'rep'))
- order: int32 [32, 64], P('feat'), may hold values from 0 to 63, each once within a row
- sweeps: int32 [2048], P('feat'), may hold values from 1 to 3
Outputs:
- direction: float32 [524288], P(('feat', 'samp', 'rep'))
- margin_change: float32 [65536], P(('samp', 'rep'))
- decrease: float32 [1], replicated
Inputs may be any that keep to these rules, and one draw needn't show every extreme that they name: `tile_block`: in every group the live slots come first and the rest hold -1; at least half of the 32 slots of every group are live, and some group has all live.
All inputs are finite; a program needn't handle non-finite values. No bound on the sum of `labels` on one device may be relied on, other than what follows from the above.
Results may differ from a plain program's by a relative error of at most 0.029.
Values may be sent and summed in bfloat16 or wider, within the bound.
A program may use at most 128 MiB of HBM per device.

v0:
```python
import jax
import jax.numpy as jnp
from jax import lax
from jax.sharding import PartitionSpec as P

SWEEPS = 3
SEGMENTS = 2


penalty = 0.05
ridge_term = 0.1


def on_device(tiles, tile_block, tile_row, labels, weights, hess_inv, order, sweeps):
    slots = tiles.shape[2]
    tile_rows = tiles.shape[3]
    width = tiles.shape[4]
    tile_data = tiles.reshape(slots, tile_rows, width)
    block_ids = tile_block.reshape(slots)
    row_ids = tile_row.reshape(slots)
    local_blocks = weights.shape[0] // width
    owned = hess_inv.shape[0]
    row_total = labels.shape[0]
    row_groups = row_total // tile_rows
    per_segment = local_blocks // SEGMENTS
    live_slot = block_ids >= 0
    safe_ids = jnp.maximum(block_ids, 0)
    block_hot = (block_ids[:, None] == jnp.arange(local_blocks)[None, :]).astype(jnp.float32)
    row_match = row_ids[:, None] == jnp.arange(row_groups)[None, :]
    row_hot = jnp.where(live_slot[:, None], row_match, False).astype(jnp.float32)

    def partial_margin(vectors):
        chosen = vectors[safe_ids]
        partial_value = jnp.einsum(
            "ctk,ck->ct", tile_data, chosen, preferred_element_type=jnp.float32
        )
        return jnp.einsum(
            "ct,cr->rt", partial_value, row_hot, precision=lax.Precision.HIGHEST
        ).reshape(row_total)

    def tile_gradient(rows_bf):
        picked = rows_bf.reshape(row_groups, tile_rows)[row_ids]
        contrib = jnp.einsum("ctk,ct->ck", tile_data, picked, preferred_element_type=jnp.float32)
        return jnp.dot(block_hot.T, contrib, precision=lax.Precision.HIGHEST)

    def reduce_rows(partial_rows):
        return lax.psum(partial_rows, "feat")

    row_weight = jnp.where(lax.axis_index("feat") == 0, 1.0, 0.0).astype(jnp.float32)
    block_weights = weights.reshape(local_blocks, width)
    margins = reduce_rows(partial_margin(block_weights.astype(jnp.bfloat16)))
    probability = jax.nn.sigmoid(margins)
    curvature = probability * (1.0 - probability)
    resid_bf = (probability - labels.astype(jnp.float32)).astype(jnp.bfloat16)
    gradient_own = lax.psum_scatter(
        tile_gradient(resid_bf), ("samp", "rep"), scatter_dimension=0, tiled=True
    )
    member = lax.axis_index(("samp", "rep"))
    first_block = member * owned
    w_own = lax.dynamic_slice_in_dim(block_weights, first_block, owned, 0)
    threshold = penalty * jnp.diagonal(hess_inv, axis1=1, axis2=2)
    matches = order[0][:, None] == jnp.arange(local_blocks)[None, :]
    positions = jnp.sum(jnp.where(matches, jnp.arange(local_blocks)[:, None], 0), axis=0)
    segment_of = positions // per_segment
    own_segment = lax.dynamic_slice_in_dim(segment_of, first_block, owned, 0)
    own_sweeps = lax.dynamic_slice_in_dim(sweeps, first_block, owned, 0)

    def curvature_part(change):
        scaled = (curvature * change).astype(jnp.bfloat16)
        terms = tile_gradient(scaled)
        return lax.psum_scatter(terms, ("samp", "rep"), scatter_dimension=0, tiled=True)

    def one_segment(step_index, state_pair, opening):
        direction, change = state_pair
        sweep_index = step_index // SEGMENTS
        segment_index = step_index % SEGMENTS
        if opening:
            hess_part = jnp.zeros((owned, width), jnp.float32)
        else:
            hess_part = curvature_part(change)
        model_grad = gradient_own + hess_part + ridge_term * direction
        trial_point = (
            w_own
            + direction
            - jnp.einsum("bij,bj->bi", hess_inv, model_grad, precision=lax.Precision.HIGHEST)
        )
        shrunk = jnp.sign(trial_point) * jnp.maximum(jnp.abs(trial_point) - threshold, 0.0)
        active = (own_segment == segment_index) & (sweep_index < own_sweeps)
        step_delta = jnp.where(active[:, None], shrunk - w_own - direction, 0.0)
        direction = direction + step_delta
        all_steps = lax.all_gather(
            step_delta.astype(jnp.bfloat16), ("samp", "rep"), axis=0, tiled=True
        )
        change = change + reduce_rows(partial_margin(all_steps))
        return (direction, change)

    def later_segment(step_index, state_pair):
        return one_segment(step_index, state_pair, False)

    start_pair = (jnp.zeros((owned, width), jnp.float32), jnp.zeros_like(margins))
    first_pair = one_segment(0, start_pair, True)
    direction, change = lax.fori_loop(1, SWEEPS * SEGMENTS, later_segment, first_pair)
    linear = jnp.sum(gradient_own * direction) + 0.5 * ridge_term * jnp.sum(direction * direction)
    linear = linear + penalty * jnp.sum(jnp.abs(w_own + direction) - jnp.abs(w_own))
    quadratic = row_weight * 0.5 * jnp.sum(curvature * change * change)
    totals = lax.psum((linear, quadratic), ("feat", "samp", "rep"))
    decrease = (totals[0] + totals[1]).reshape(1)
    return (direction.reshape(-1), change, decrease)


def solution(mesh):
    in_specs = (
        P("feat", ("samp", "rep"), None, None, None),
        P("feat", ("samp", "rep"), None),
        P("feat", ("samp", "rep"), None),
        P(("samp", "rep")),
        P("feat"),
        P(("feat", "samp", "rep"), None, None),
        P("feat", None),
        P("feat"),
    )
    out_specs = (P(("feat", "samp", "rep")), P(("samp", "rep")), P())
    return jax.shard_map(
        on_device, mesh=mesh, in_specs=in_specs, out_specs=out_specs, check_vma=False
    )
```

profile of v0, /device:TPU:1, one launch (start us, length us, event | category | flops | bytes accessed | tf_op | source)
XLA Modules:
  0.0 1847.5 jit_solution(16925165963029127707)
XLA Ops:
  7.2 0.8 maximum_bitcast_fusion
  8.0 0.7 broadcast_compare_fusion
  8.7 0.9 reshape.153
  9.6 0.7 fusion.49
  10.3 0.6 gather_fusion.2
  10.9 2.3 fusion.31
  13.5 116.3 %psum.42 = f32[4096]{0:T(1024)S(1)} all-reduce(f32[4096]{0:T(1024)S(1)} %convolution_bitcast_fusion.3), channel_id=1, replica_groups=mesh['feat'=32,'samp'=8,'rep'=2] {'feat'}, use_global_device_ids=true, to_apply=%region_1.2 | all-reduce | flops 4096 | bytes 32768 | tf_op jit(solution)/shard_map/psum | solution.py:47
  130.8 0.9 fusion.26
  132.3 16.5 copy.17
  148.8 2.3 gather_fusion.4
  151.4 0.6 dynamic-slice.2
  152.7 111.3 %all-reduce.7.cloned.1.call-done = f32[64,256]{1,0:T(8,128)} async-done(((f32[64,256]{1,0:T(8,128)}), f32[64,256]{1,0:T(8,128)}) %all-reduce.7.cloned.1.call-update) | async-done | bytes 65552
  264.0 0.7 fusion.62
  264.7 1.0 fusion.47
  265.8 15.1 all-gather.1
  280.9 0.6 gather_fusion.5
  281.5 0.6 fusion.28
  282.2 0.9 convolution_bitcast_fusion.2
  283.1 115.1 %psum.43 = f32[4096]{0:T(1024)S(1)} all-reduce(f32[4096]{0:T(1024)S(1)} %convolution_bitcast_fusion.2), channel_id=1, replica_groups=mesh['feat'=32,'samp'=8,'rep'=2] {'feat'}, use_global_device_ids=true, to_apply=%region_3.4 | all-reduce | flops 4096 | bytes 32768 | tf_op jit(solution)/shard_map/psum | solution.py:47
  398.2 0.7 constant_dynamic-slice_fusion
  398.9 1316.2 %while.19 = (s32[]{:T(128)}, f32[4,256]{1,0:T(4,128)S(1)}, f32[4096]{0:T(1024)S(1)}, s32[4]{0:T(128)S(1)}, s32[4]{0:T(128)S(1)}, /*index=5*/f32[4,256]{1,0:T(4,1...) while((s32[]{:T(128)}, f32[4,256]{1,0:T(4,128)S(1)}, ...), condition=%wide.region_7.8_spmd.clone.clone, body=%wide.region_4.7_spmd.clone.clone.sunk | while | flops 15261924 | bytes 6182700 | solution.py:102
  400.0 0.9 convolution_bitcast_fusion.6
  402.3 126.5 %all-reduce.9.cloned.1.call-done = f32[64,256]{1,0:T(8,128)} async-done(((f32[64,256]{1,0:T(8,128)}), f32[64,256]{1,0:T(8,128)}) %all-reduce.9.cloned.1.call-update) | async-done | bytes 65552 | tf_op jit(solution)/shard_map/while
  528.8 0.7 fusion.93
  529.5 1.0 fusion.94
  530.6 15.1 all-gather.5
  545.7 0.6 gather_fusion.1
  546.3 0.6 fusion.96
  547.2 115.1 %psum.50 = f32[4096]{0:T(1024)S(1)} all-reduce(f32[4096]{0:T(1024)S(1)} %convolution_bitcast_fusion.7), channel_id=1, replica_groups=mesh['feat'=32,'samp'=8,'rep'=2] {'feat'}, use_global_device_ids=true, to_apply=%region_6.6 | all-reduce | flops 4096 | bytes 32768 | tf_op jit(solution)/shard_map/while/body/eval_jaxpr/psum | solution.py:47
  663.4 0.9 convolution_bitcast_fusion.6
  665.7 126.6 %all-reduce.9.cloned.1.call-done = f32[64,256]{1,0:T(8,128)} async-done(((f32[64,256]{1,0:T(8,128)}), f32[64,256]{1,0:T(8,128)}) %all-reduce.9.cloned.1.call-update) | async-done | bytes 65552 | tf_op jit(solution)/shard_map/while
  792.2 0.7 fusion.93
  792.9 1.0 fusion.94
  794.0 15.1 all-gather.5
  809.1 0.6 gather_fusion.1
  809.7 0.6 fusion.96
  810.6 115.1 %psum.50 = f32[4096]{0:T(1024)S(1)} all-reduce(f32[4096]{0:T(1024)S(1)} %convolution_bitcast_fusion.7), channel_id=1, replica_groups=mesh['feat'=32,'samp'=8,'rep'=2] {'feat'}, use_global_device_ids=true, to_apply=%region_6.6 | all-reduce | flops 4096 | bytes 32768 | tf_op jit(solution)/shard_map/while/body/eval_jaxpr/psum | solution.py:47
  926.8 0.9 convolution_bitcast_fusion.6
  929.1 126.3 %all-reduce.9.cloned.1.call-done = f32[64,256]{1,0:T(8,128)} async-done(((f32[64,256]{1,0:T(8,128)}), f32[64,256]{1,0:T(8,128)}) %all-reduce.9.cloned.1.call-update) | async-done | bytes 65552 | tf_op jit(solution)/shard_map/while
  1055.3 0.7 fusion.93
  1056.0 1.0 fusion.94
  1057.1 15.1 all-gather.5
  1072.2 0.6 gather_fusion.1
  1072.8 0.6 fusion.96
  1073.8 115.1 %psum.50 = f32[4096]{0:T(1024)S(1)} all-reduce(f32[4096]{0:T(1024)S(1)} %convolution_bitcast_fusion.7), channel_id=1, replica_groups=mesh['feat'=32,'samp'=8,'rep'=2] {'feat'}, use_global_device_ids=true, to_apply=%region_6.6 | all-reduce | flops 4096 | bytes 32768 | tf_op jit(solution)/shard_map/while/body/eval_jaxpr/psum | solution.py:47
  1189.9 0.9 convolution_bitcast_fusion.6
  1192.2 126.3 %all-reduce.9.cloned.1.call-done = f32[64,256]{1,0:T(8,128)} async-done(((f32[64,256]{1,0:T(8,128)}), f32[64,256]{1,0:T(8,128)}) %all-reduce.9.cloned.1.call-update) | async-done | bytes 65552 | tf_op jit(solution)/shard_map/while
  1318.4 0.7 fusion.93
  1319.1 1.0 fusion.94
  1320.2 15.1 all-gather.5
  1335.3 0.6 gather_fusion.1
  1336.0 0.6 fusion.96
  1336.9 115.1 %psum.50 = f32[4096]{0:T(1024)S(1)} all-reduce(f32[4096]{0:T(1024)S(1)} %convolution_bitcast_fusion.7), channel_id=1, replica_groups=mesh['feat'=32,'samp'=8,'rep'=2] {'feat'}, use_global_device_ids=true, to_apply=%region_6.6 | all-reduce | flops 4096 | bytes 32768 | tf_op jit(solution)/shard_map/while/body/eval_jaxpr/psum | solution.py:47
  1453.0 0.9 convolution_bitcast_fusion.6
  1455.3 126.3 %all-reduce.9.cloned.1.call-done = f32[64,256]{1,0:T(8,128)} async-done(((f32[64,256]{1,0:T(8,128)}), f32[64,256]{1,0:T(8,128)}) %all-reduce.9.cloned.1.call-update) | async-done | bytes 65552 | tf_op jit(solution)/shard_map/while
  1581.6 0.7 fusion.93
  1582.3 1.0 fusion.94
  1583.3 15.1 all-gather.5
  1598.4 0.6 gather_fusion.1
  1599.1 0.6 fusion.96
  1600.0 115.1 %psum.50 = f32[4096]{0:T(1024)S(1)} all-reduce(f32[4096]{0:T(1024)S(1)} %convolution_bitcast_fusion.7), channel_id=1, replica_groups=mesh['feat'=32,'samp'=8,'rep'=2] {'feat'}, use_global_device_ids=true, to_apply=%region_6.6 | all-reduce | flops 4096 | bytes 32768 | tf_op jit(solution)/shard_map/while/body/eval_jaxpr/psum | solution.py:47
  1715.1 1.4 subtract_reduce_fusion
  1717.8 0.6 fusion.33
  1720.4 120.3 %psum.46 = f32[]{:T(128)} all-reduce(f32[]{:T(128)S(6)} %add.182), channel_id=1, replica_groups=mesh['feat'=32,'samp'=8,'rep'=2] {'feat','samp','rep'}, use_global_device_ids=true, to_apply=%region_11.12 | all-reduce | flops 1 | bytes 8 | tf_op jit(solution)/shard_map/psum | solution.py:106
  (123 shorter events, 13.0 us)
Async XLA Ops:
  7.2 6.1 copy-start.7
  7.2 123.2 %copy-start = (bf16[1,1,32,128,256]{4,3,2,1,0:T(8,128)(2,1)S(1)}, bf16[1,1,32,128,256]{4,3,2,1,0:T(8,128)(2,1)}, u32[]{:S(2)}) copy-start(bf16[1,1,32,128,256]{4,3,2,1,0:T(8,128)(2,1)} %param.10) | copy-start | bytes 6291460
  7.2 122.6 %copy-start.3 = (s32[4096]{0:T(1024)S(1)}, s32[4096]{0:T(1024)}, u32[]{:S(2)}) copy-start(s32[4096]{0:T(1024)} %param.13) | copy-start | bytes 49156
  7.2 256.8 %all-reduce.7.cloned.1.call-start = ((), (), s32[]{:S(2)}) async-start(), calls=%async_computation | async-start | bytes 131072
  8.7 121.1 %copy-start.9 = (pred[32]{0:T(512)(128)(4,1)}, pred[32]{0:T(512)(128)(4,1)S(1)}, u32[]{:S(2)}) copy-start(pred[32]{0:T(512)(128)(4,1)S(1)} %broadcast_compare_fusion) | copy-start | bytes 100
  10.9 119.9 %copy-start.4 = (s32[1,1,32]{2,1,0:T(1,128)S(1)}, s32[1,1,32]{2,1,0:T(1,128)}, u32[]{:S(2)}) copy-start(s32[1,1,32]{2,1,0:T(1,128)} %param.11) | copy-start | bytes 388
  10.9 121.4 %copy-start.1 = (f32[4,256,256]{2,1,0:T(8,128)S(1)}, f32[4,256,256]{2,1,0:T(8,128)}, u32[]{:S(2)}) copy-start(f32[4,256,256]{2,1,0:T(8,128)} %param.15) | copy-start | bytes 3145732
  132.3 18.9 %copy-start.6 = (s32[1,64]{1,0:T(1,128)S(1)}, s32[1,64]{1,0:T(1,128)}, u32[]{:S(2)}) copy-start(s32[1,64]{1,0:T(1,128)} %param.16) | copy-start | bytes 772
  132.3 19.0 %copy-start.5 = (s32[64]{0:T(128)S(1)}, s32[64]{0:T(128)}, u32[]{:S(2)}) copy-start(s32[64]{0:T(128)} %param.17) | copy-start | bytes 772
  132.3 19.2 %copy-start.8 = (u32[512]{0:T(512)S(1)}, u32[512]{0:T(512)}, u32[]{:S(2)}) copy-start(u32[512]{0:T(512)} %constant.190) | copy-start | bytes 6148
  151.1 247.8 %copy-start.10 = (pred[32]{0:T(512)(128)(4,1)S(1)}, pred[32]{0:T(512)(128)(4,1)}, u32[]{:S(2)}) copy-start(pred[32]{0:T(512)(128)(4,1)} %copy-done.9) | copy-start | bytes 100
  151.1 247.8 %copy-start.11 = (s32[32]{0:T(128)S(1)}, s32[32]{0:T(128)}, u32[]{:S(2)}) copy-start(s32[32]{0:T(128)} %broadcast_maximum_fusion) | copy-start | bytes 388
  398.9 129.9 %all-reduce.9.cloned.1.call-start = ((), (), s32[]{:S(2)}) async-start(), calls=%async_computation.1 | async-start | bytes 131072 | tf_op jit(solution)/shard_map/while
  662.3 129.9 %all-reduce.9.cloned.1.call-start = ((), (), s32[]{:S(2)}) async-start(), calls=%async_computation.1 | async-start | bytes 131072 | tf_op jit(solution)/shard_map/while
  925.8 129.6 %all-reduce.9.cloned.1.call-start = ((), (), s32[]{:S(2)}) async-start(), calls=%async_computation.1 | async-start | bytes 131072 | tf_op jit(solution)/shard_map/while
  1188.9 129.6 %all-reduce.9.cloned.1.call-start = ((), (), s32[]{:S(2)}) async-start(), calls=%async_computation.1 | async-start | bytes 131072 | tf_op jit(solution)/shard_map/while
  1452.0 129.6 %all-reduce.9.cloned.1.call-start = ((), (), s32[]{:S(2)}) async-start(), calls=%async_computation.1 | async-start | bytes 131072 | tf_op jit(solution)/shard_map/while
  1715.1 125.6 %copy-start.2 = (f32[4096]{0:T(1024)}, f32[4096]{0:T(1024)S(1)}, u32[]{:S(2)}) copy-start(f32[4096]{0:T(1024)S(1)} %get-tuple-element.357) | copy-start | bytes 49156
Sparse Core Ops, SparseCore 0:
  131.9 132.1 all-reduce.6
  402.2 126.5 all-reduce.8
  665.6 126.5 all-reduce.8
  928.7 126.5 all-reduce.8
  1191.8 126.5 all-reduce.8
  1454.9 126.5 all-reduce.8
where the time goes:
time: 1850 us
  blocking collectives  1020 us (55%)
  waiting for transfers between devices  743 us (40%)
  local copies, waits for them, and re-layouts  33.4 us (2%)
  matrix products  22.5 us (1%)
    psum x7, blocking collectives, reduce_rows(): return lax.psum(partial_rows, 'feat')  807 us
    while x10, waiting for transfers between devices  632 us
    psum x1, blocking collectives, on_device(): totals = lax.psum((linear, quadratic), ('feat', 'samp', 'rep'))  120 us
    unnamed x2, waiting for transfers between devices  111 us
    all_gather x6, blocking collectives, one_segment(): lax.all_gather(step_delta.astype(jnp.bfloat16), ('samp', 'rep'), axis=0,...  90.6 us
  transfers between devices with their start and end apart: 6, of which 6 were waited for; matrix products, arithmetic and copies ran while one was open for 1% of the time, Pallas kernels for 0%

commit v1 on v0

v1 whole, which is shorter than its diff:
```python
import functools

import jax
import jax.numpy as jnp
from jax import lax
from jax.experimental import pallas as pl
from jax.experimental.pallas import tpu as pltpu
from jax.sharding import PartitionSpec as P

SWEEPS = 3
SEGMENTS = 2
ROUNDS = SWEEPS * SEGMENTS

NX = 4
NY = 8
NM = 16
SLOTS = 32
TILE_ROWS = 128
WIDTH = 256
HALF = 128
GROUPS = 32
BLOCKS = 64
OWNED = 4

penalty = 0.05
ridge_term = 0.1

MESH = pl.DeviceIdType.MESH
F32 = jnp.float32
BF16 = jnp.bfloat16


def far_first(count, chips):
    per = count // chips
    return sorted(range(1, count), key=lambda j: -min(j // per, chips - j // per))


def iota(shape, dim):
    return lax.broadcasted_iota(jnp.int32, shape, dim)


def body(
    tile_block,
    tile_row,
    order,
    sweeps,
    tiles,
    labels,
    weights,
    hess,
    dir_out,
    change_out,
    dec_out,
    tiles_t,
    hess_t,
    vecs,
    rows,
    q_buf,
    p_buf,
    thr,
    w_own,
    grad,
    direc,
    curv,
    x_buf,
    y_buf,
    rs_out,
    rs_in,
    ag_buf,
    lx_buf,
    ly_buf,
    lz_buf,
    x_send,
    x_recv,
    y_send,
    y_recv,
    z_send,
    z_recv,
    l_send,
    l_recv,
):
    f, s, r = lax.axis_index("feat"), lax.axis_index("samp"), lax.axis_index("rep")
    me_x, me_y = f % NX, f // NX
    me = s * 2 + r

    def x_dev(j):
        return (me_y * NX + (me_x + j) % NX, s, r)

    def y_dev(j):
        return ((me_y + j) % NY * NX + me_x, s, r)

    def z_dev(j):
        return (f, (s + j // 2) % 8, r ^ (j % 2))

    barrier = pltpu.get_barrier_semaphore()
    for dev, count in ((x_dev, NX), (y_dev, NY), (z_dev, NM)):
        for j in range(1, count):
            pl.semaphore_signal(barrier, inc=1, device_id=dev(j), device_id_type=MESH)

    for m in range(NM):
        vecs[8 * m : 8 * m + 4] = weights[pl.ds(8 * m, 4, stride=2)]
        vecs[8 * m + 4 : 8 * m + 8] = weights[pl.ds(8 * m + 1, 4, stride=2)]
    w_own[...] = vecs[pl.ds(pl.multiple_of(me * 8, 8), 8)]
    direc[...] = jnp.zeros((8, HALF), F32)
    change_out[...] = jnp.zeros((GROUPS, TILE_ROWS), F32)

    def flip_tile(c, carry):
        tiles_t[c] = tiles[c].T
        return carry

    lax.fori_loop(0, SLOTS, flip_tile, 0, unroll=4)

    def flip_hess(i, carry):
        block = hess[i]
        flipped = block.T
        high = flipped.astype(BF16)
        hess_t[i] = high
        hess_t[OWNED + i] = (flipped - high.astype(F32)).astype(BF16)
        on_diag = iota((WIDTH, WIDTH), 0) == iota((WIDTH, WIDTH), 1)
        diagonal = jnp.sum(jnp.where(on_diag, block, 0.0), axis=0, keepdims=True)
        thr[pl.ds(i, 1)] = penalty * diagonal[:, :HALF]
        thr[pl.ds(OWNED + i, 1)] = penalty * diagonal[:, HALF:]
        return carry

    lax.fori_loop(0, OWNED, flip_hess, 0)

    sub = iota((8, HALF), 0) % OWNED
    first_half = jnp.zeros((8, HALF), jnp.int32)
    limit = jnp.zeros((8, HALF), jnp.int32)
    for i in range(OWNED):
        own_block = me * OWNED + i
        found = jnp.int32(0)
        for p in range(BLOCKS // SEGMENTS):
            found = found + jnp.where(order[0, p] == own_block, 1, 0)
        first_half = jnp.where(sub == i, found, first_half)
        limit = jnp.where(sub == i, sweeps[own_block], limit)
    own_segment = 1 - first_half

    pl.semaphore_wait(barrier, NX + NY + NM - 3)

    row_iota = iota((GROUPS, HALF), 0)
    block_iota = iota((BLOCKS, TILE_ROWS), 0)

    def forward():
        def fill(c, carry):
            b = tile_block[0, 0, c]
            live = b >= 0
            b = jnp.maximum(b, 0)
            at = 8 * (b // 4) + b % 4
            group = jnp.where(live, tile_row[0, 0, c], -1)
            hot = row_iota == group
            left = jnp.where(hot, vecs[pl.ds(at, 1)], 0.0).astype(BF16)
            right = jnp.where(hot, vecs[pl.ds(at + 4, 1)], 0.0).astype(BF16)
            base = pl.multiple_of(c * WIDTH, WIDTH)
            q_buf[:, pl.ds(base, HALF)] = left
            q_buf[:, pl.ds(base + HALF, HALF)] = right
            return carry

        lax.fori_loop(0, SLOTS, fill, 0, unroll=True)
        flipped = tiles_t[...].reshape(SLOTS * WIDTH, TILE_ROWS)
        return jnp.dot(q_buf[...], flipped, preferred_element_type=F32)

    def backward():
        def fill(c, carry):
            b = tile_block[0, 0, c]
            picked = rows[pl.ds(tile_row[0, 0, c], 1)]
            base = pl.multiple_of(c * TILE_ROWS, TILE_ROWS)
            p_buf[:, pl.ds(base, TILE_ROWS)] = jnp.where(block_iota == b, picked, 0.0).astype(BF16)
            return carry

        lax.fori_loop(0, SLOTS, fill, 0, unroll=True)
        flat = tiles[...].reshape(SLOTS * TILE_ROWS, WIDTH)
        return jnp.dot(p_buf[...], flat, preferred_element_type=F32)

    def send(src, dst, send_sem, recv_sem, dev):
        pltpu.make_async_remote_copy(
            src_ref=src,
            dst_ref=dst,
            send_sem=send_sem,
            recv_sem=recv_sem,
            device_id=dev,
            device_id_type=MESH,
        ).start()

    def drain(ref, sem):
        pltpu.make_async_copy(ref, ref, sem).wait()

    def line_start(buf, value, me_at, count, send_sem, recv_sem, dev):
        buf[me_at] = value
        for j in far_first(count, min(count, 8)):
            send(buf.at[me_at], buf.at[me_at], send_sem, recv_sem, dev(j))

    def line_finish(buf, count, send_sem, recv_sem):
        drain(buf.at[pl.ds(0, count - 1)], recv_sem)
        total = buf[0].astype(F32)
        for k in range(1, count):
            total = total + buf[k].astype(F32)
        drain(buf.at[pl.ds(0, count - 1)], send_sem)
        return total

    def reduce_rows(part, slot):
        xb, yb = x_buf.at[slot], y_buf.at[slot]
        xs, xr, ys, yr = x_send.at[slot], x_recv.at[slot], y_send.at[slot], y_recv.at[slot]
        line_start(xb, part.astype(BF16), me_x, NX, xs, xr, x_dev)
        total = line_finish(xb, NX, xs, xr)
        line_start(yb, total.astype(BF16), me_y, NY, ys, yr, y_dev)
        return line_finish(yb, NY, ys, yr)

    def one_round(t, carry):
        summed = reduce_rows(forward(), t % 2)

        @pl.when(t == 0)
        def _():
            prob = jax.nn.sigmoid(summed)
            curv[...] = prob * (1.0 - prob)
            rows[...] = prob - labels[...].astype(F32)

        @pl.when(t > 0)
        def _():
            change = change_out[...] + summed
            change_out[...] = change
            rows[...] = curv[...] * change

        contrib = backward()
        for m in range(NM):
            rs_out[m] = jnp.concatenate(
                [
                    contrib[OWNED * m : OWNED * (m + 1), :HALF],
                    contrib[OWNED * m : OWNED * (m + 1), HALF:],
                ],
                axis=0,
            )
        for j in far_first(NM, 8):
            dev = z_dev(j)
            send(rs_out.at[dev[1] * 2 + dev[2]], rs_in.at[j - 1], z_send.at[0], z_recv.at[0], dev)
        mine = rs_out[me]
        drain(rs_in, z_recv.at[0])
        for j in range(NM - 1):
            mine = mine + rs_in[j]
        drain(rs_in, z_send.at[0])

        @pl.when(t == 0)
        def _():
            grad[...] = mine

        direction = direc[...]
        model_grad = grad[...] + jnp.where(t > 0, mine, 0.0) + ridge_term * direction
        wide = jnp.concatenate([model_grad[:OWNED], model_grad[OWNED:]], axis=1)
        high = wide.astype(BF16).astype(F32)
        pair = jnp.concatenate([high, wide - high, jnp.zeros((8, WIDTH), F32)], axis=0)
        at = iota((16, WIDTH), 0)
        parts = [jnp.where(at % OWNED == i, pair, 0.0) for i in range(OWNED)]
        parts += [jnp.where(at == i, pair, 0.0) for i in range(OWNED)]
        spread = jnp.concatenate(parts, axis=1).astype(BF16)
        product = jnp.dot(
            spread, hess_t[...].reshape(2 * OWNED * WIDTH, WIDTH), preferred_element_type=F32
        )
        product = product[:OWNED] + product[OWNED : 2 * OWNED]
        newton = jnp.concatenate([product[:, :HALF], product[:, HALF:]], axis=0)
        weight = w_own[...]
        trial = weight + direction - newton
        size = jnp.maximum(jnp.abs(trial) - thr[...], 0.0)
        shrunk = jnp.where(trial > 0.0, size, jnp.where(trial < 0.0, -size, 0.0))
        active = (own_segment == t % SEGMENTS) & (t // SEGMENTS < limit)
        step = jnp.where(active, shrunk - weight - direction, 0.0)
        direc[...] = direction + step

        slot = ag_buf.at[pl.ds(pl.multiple_of(me * 8, 8), 8)]
        slot[...] = step
        for j in far_first(NM, 8):
            send(slot, slot, z_send.at[1], z_recv.at[1], z_dev(j))
        drain(ag_buf.at[pl.ds(0, 8 * (NM - 1))], z_recv.at[1])
        vecs[...] = ag_buf[...]
        drain(ag_buf.at[pl.ds(0, 8 * (NM - 1))], z_send.at[1])
        return carry

    lax.fori_loop(0, ROUNDS, one_round, 0)

    direction = direc[...]
    weight = w_own[...]
    linear = grad[...] * direction + 0.5 * ridge_term * direction * direction
    linear = linear + penalty * (jnp.abs(weight + direction) - jnp.abs(weight))
    line_start(lx_buf, linear, me_x, NX, l_send.at[0], l_recv.at[0], x_dev)
    part = forward()
    linear = line_finish(lx_buf, NX, l_send.at[0], l_recv.at[0])
    line_start(ly_buf, linear, me_y, NY, l_send.at[1], l_recv.at[1], y_dev)
    summed = reduce_rows(part, ROUNDS % 2)
    change = change_out[...] + summed
    linear = line_finish(ly_buf, NY, l_send.at[1], l_recv.at[1])
    quad = 0.5 * curv[...] * change * change
    for g in range(GROUPS // 8):
        linear = linear + quad[8 * g : 8 * g + 8]
    line_start(lz_buf, linear, me, NM, l_send.at[2], l_recv.at[2], z_dev)
    change_out[...] = change
    dir_out[pl.ds(0, OWNED, stride=2)] = direction[:OWNED]
    dir_out[pl.ds(1, OWNED, stride=2)] = direction[OWNED:]
    total = line_finish(lz_buf, NM, l_send.at[2], l_recv.at[2])
    dec_out[...] = jnp.sum(jnp.sum(total, axis=0, keepdims=True), axis=1, keepdims=True)


def on_device(tiles, tile_block, tile_row, labels, weights, hess_inv, order, sweeps):
    smem = pl.BlockSpec(memory_space=pltpu.SMEM)
    vmem = pl.BlockSpec(memory_space=pltpu.VMEM)
    dma = pltpu.SemaphoreType.DMA
    direction, change, decrease = pl.pallas_call(
        body,
        out_shape=(
            jax.ShapeDtypeStruct((8, HALF), F32),
            jax.ShapeDtypeStruct((GROUPS, TILE_ROWS), F32),
            jax.ShapeDtypeStruct((1, 1), F32),
        ),
        in_specs=[smem] * 4 + [vmem] * 4,
        out_specs=[vmem] * 3,
        scratch_shapes=[
            pltpu.VMEM((SLOTS, WIDTH, TILE_ROWS), BF16),
            pltpu.VMEM((2 * OWNED, WIDTH, WIDTH), BF16),
            pltpu.VMEM((8 * NM, HALF), F32),
            pltpu.VMEM((GROUPS, TILE_ROWS), F32),
            pltpu.VMEM((GROUPS, SLOTS * WIDTH), BF16),
            pltpu.VMEM((BLOCKS, SLOTS * TILE_ROWS), BF16),
            pltpu.VMEM((8, HALF), F32),
            pltpu.VMEM((8, HALF), F32),
            pltpu.VMEM((8, HALF), F32),
            pltpu.VMEM((8, HALF), F32),
            pltpu.VMEM((GROUPS, TILE_ROWS), F32),
            pltpu.VMEM((2, NX, GROUPS, TILE_ROWS), BF16),
            pltpu.VMEM((2, NY, GROUPS, TILE_ROWS), BF16),
            pltpu.VMEM((NM, 8, HALF), F32),
            pltpu.VMEM((NM - 1, 8, HALF), F32),
            pltpu.VMEM((8 * NM, HALF), F32),
            pltpu.VMEM((NX, 8, HALF), F32),
            pltpu.VMEM((NY, 8, HALF), F32),
            pltpu.VMEM((NM, 8, HALF), F32),
            dma((2,)),
            dma((2,)),
            dma((2,)),
            dma((2,)),
            dma((2,)),
            dma((2,)),
            dma((3,)),
            dma((3,)),
        ],
        compiler_params=pltpu.CompilerParams(
            collective_id=0, has_side_effects=True, vmem_limit_bytes=40 * 1024 * 1024
        ),
    )(
        tile_block,
        tile_row,
        order,
        sweeps,
        tiles.reshape(SLOTS, TILE_ROWS, WIDTH),
        labels.reshape(GROUPS, TILE_ROWS),
        weights.reshape(2 * BLOCKS, HALF),
        hess_inv,
    )
    return direction.reshape(-1), change.reshape(-1), decrease.reshape(1)


def solution(mesh):
    in_specs = (
        P("feat", ("samp", "rep"), None, None, None),
        P("feat", ("samp", "rep"), None),
        P("feat", ("samp", "rep"), None),
        P(("samp", "rep")),
        P("feat"),
        P(("feat", "samp", "rep"), None, None),
        P("feat", None),
        P("feat"),
    )
    out_specs = (P(("feat", "samp", "rep")), P(("samp", "rep")), P())
    return jax.shard_map(
        on_device, mesh=mesh, in_specs=in_specs, out_specs=out_specs, check_vma=False
    )
```

time: 1850 us -> 156 us (0.08)
  blocking collectives: 1020 us -> 0 us
  waiting for transfers between devices: 743 us -> 0 us
  Pallas kernels: 0 us -> 145 us
  local copies, waits for them, and re-layouts: 33.4 us -> 8.18 us
  matrix products: 22.5 us -> 0 us
    psum x8 -> x0, blocking collectives: 927 us -> none  [the longest x7 807 us: reduce_rows(): return lax.psum(partial_rows, 'feat')]
    while x10 -> x0, waiting for transfers between devices: 632 us -> none
    pallas_call x0 -> x1, Pallas kernels: none -> 145 us  [on_device(): pl.pallas_call(body, out_shape=(jax.ShapeDtypeStruct((8, HALF), F32), jax...]
    unnamed x2 -> x0, waiting for transfers between devices: 111 us -> none
    all_gather x6 -> x0, blocking collectives: 90.6 us -> none  [one_segment(): lax.all_gather(step_delta.astype(jnp.bfloat16), ('samp', 'rep'), axis=0,...]
    dot_general x32 -> x0, matrix products: 22.5 us -> none  [the longest x7 6.13 us: partial_margin(): jnp.einsum('ctk,ck->ct', tile_data, chosen, preferred_element_type=jnp.fl...]
  transfers between devices with their start and end apart: 6 -> 0, of which waited for: 6 -> 0; matrix products, arithmetic and copies ran while one was open for 1% -> 0% of each run, Pallas kernels for 0% -> 0%
where the time goes in v1:
time: 156 us
  Pallas kernels  145 us (93%)
  local copies, waits for them, and re-layouts  8.18 us (5%)
  between operations  2.47 us (2%)
    pallas_call x1, Pallas kernels, on_device(): pl.pallas_call(body, out_shape=(jax.ShapeDtypeStruct((8, HALF), F32), jax...  145 us
    unnamed x18, local copies, waits for them, and re-layouts  8.18 us

profile of v1, /device:TPU:1, one launch (start us, length us, event | category | flops | bytes accessed | tf_op | source)
XLA Modules:
  0.0 156.1 jit_solution(7665119624689341132)
XLA Ops:
  0.6 0.0 copy-start
  0.6 1.6 %copy-done = bf16[1,1,32,128,256]{4,3,2,1,0:T(8,128)(2,1)S(1)} copy-done((bf16[1,1,32,128,256]{4,3,2,1,0:T(8,128)(2,1)S(1)}, bf16[1,1,32,128,256]{4,3,2,1,0:T(8,128)(2,1)}, u32[]{:S(2)}) %copy-start) | copy-done | bytes 2097176
  2.2 0.0 copy-start.1
  2.2 1.2 copy-done.1
  3.5 0.0 copy-start.2
  3.5 0.8 copy-done.2
  4.3 0.0 copy-start.3
  4.3 0.7 copy-done.3
  5.0 0.0 copy-start.4
  5.0 0.7 copy-done.4
  5.7 0.0 copy-start.5
  5.7 0.7 copy-done.5
  6.3 0.0 copy-start.6
  6.3 0.7 copy-done.6
  7.0 0.0 copy-start.7
  7.0 0.7 copy-done.7
  7.6 145.4 %shard_map.103 = (f32[8,128]{1,0:T(8,128)S(1)}, f32[32,128]{1,0:T(8,128)S(1)}, f32[1,1]{1,0:T(1,128)}) custom-call(s32[1,1,32]{2,1,0:T(1,128)S(1)} %copy-done.4, s32[1,1,32]{2,1,0:T(1,128)S(1)} %copy-done.5, s32[1,64]{1,0:T(1,128)S(1)} %copy-done.6, s32[64]{0:T(128)S(1)} %copy-done.7, bf16[32,128,256]{2,1,0:T(8,128)(2,1)S(1)} %bitcast.6, ...), custom_call_target="tpu_custom_call" | custom-call | tf_op jit(solution)/shard_map/pallas_call | solution.py:305
  153.0 0.6 copy.14
  153.6 0.6 copy.15
Async XLA Ops:
  0.6 1.6 %copy-start = (bf16[1,1,32,128,256]{4,3,2,1,0:T(8,128)(2,1)S(1)}, bf16[1,1,32,128,256]{4,3,2,1,0:T(8,128)(2,1)}, u32[]{:S(2)}) copy-start(bf16[1,1,32,128,256]{4,3,2,1,0:T(8,128)(2,1)} %param.8) | copy-start | bytes 6291460
  2.2 1.2 copy-start.1
  3.5 0.8 copy-start.2
  4.3 0.7 copy-start.3
  5.0 0.7 copy-start.4
  5.7 0.7 copy-start.5
  6.3 0.7 copy-start.6
  7.0 0.7 copy-start.7

commit v2 on v1

v2 whole, which is shorter than its diff:
```python
import functools

import jax
import jax.numpy as jnp
from jax import lax
from jax.experimental import pallas as pl
from jax.experimental.pallas import tpu as pltpu
from jax.sharding import PartitionSpec as P

SWEEPS = 3
SEGMENTS = 2
ROUNDS = SWEEPS * SEGMENTS

NX = 4
NY = 8
NZ = 8
NM = 16
SLOTS = 32
TILE_ROWS = 128
WIDTH = 256
HALF = 128
GROUPS = 32
BLOCKS = 64
OWNED = 8
SHARE = 4
PIECES = 4

penalty = 0.05
ridge_term = 0.1

MESH = pl.DeviceIdType.MESH
F32 = jnp.float32
BF16 = jnp.bfloat16


def far_first(count, chips):
    per = count // chips
    return sorted(range(1, count), key=lambda j: -min(j // per, chips - j // per))


def iota(shape, dim):
    return lax.broadcasted_iota(jnp.int32, shape, dim)


def body(
    tile_block_hbm,
    tile_row_hbm,
    order_hbm,
    sweeps_hbm,
    tiles_hbm,
    labels_hbm,
    weights_hbm,
    hess_hbm,
    dir_out,
    change_out,
    dec_out,
    tile_block,
    tile_row,
    order,
    sweeps,
    tiles,
    labels,
    weights,
    hess,
    tiles_t,
    hess_t,
    vecs,
    rows,
    q_buf,
    p_buf,
    thr,
    w_own,
    grad,
    direc,
    segment,
    limit,
    curv,
    x_buf,
    y_buf,
    rs_out,
    rs_in,
    ag_buf,
    lx_buf,
    ly_buf,
    lz_buf,
    x_send,
    x_recv,
    y_send,
    y_recv,
    z_send,
    z_recv,
    l_send,
    l_recv,
    h_send,
    h_recv,
    load_sem,
):
    f, s, r = lax.axis_index("feat"), lax.axis_index("samp"), lax.axis_index("rep")
    me_x, me_y = f % NX, f // NX
    me = s * 2 + r

    def x_dev(j):
        return (me_y * NX + (me_x + j) % NX, s, r)

    def y_dev(j):
        return ((me_y + j) % NY * NX + me_x, s, r)

    def z_dev(j):
        return (f, (s + j // 2) % NZ, r ^ (j % 2))

    def z_same(j):
        return (f, (s + j) % NZ, r)

    def load(src, dst, k):
        return pltpu.make_async_copy(src, dst, load_sem.at[k])

    loads = [
        load(tile_block_hbm, tile_block, 0),
        load(tile_row_hbm, tile_row, 1),
        load(weights_hbm, weights, 2),
    ]
    per_piece = SLOTS // PIECES
    pieces = [
        load(
            tiles_hbm.at[pl.ds(k * per_piece, per_piece)],
            tiles.at[pl.ds(k * per_piece, per_piece)],
            3 + k,
        )
        for k in range(PIECES)
    ]
    later = [
        load(hess_hbm, hess, 3 + PIECES),
        load(labels_hbm, labels, 4 + PIECES),
        load(order_hbm, order, 5 + PIECES),
        load(sweeps_hbm, sweeps, 6 + PIECES),
    ]
    for copy in loads + pieces + later:
        copy.start()

    barrier = pltpu.get_barrier_semaphore()
    for dev, count in ((x_dev, NX), (y_dev, NY), (z_dev, NM)):
        for j in range(1, count):
            pl.semaphore_signal(barrier, inc=1, device_id=dev(j), device_id_type=MESH)

    row_iota = iota((GROUPS, HALF), 0)
    block_iota = iota((BLOCKS, TILE_ROWS), 0)

    def fill_forward():
        def fill(c, carry):
            b = tile_block[0, 0, c]
            live = b >= 0
            b = jnp.maximum(b, 0)
            at = 2 * OWNED * (b // OWNED) + b % OWNED
            group = jnp.where(live, tile_row[0, 0, c], -1)
            hot = row_iota == group
            left = jnp.where(hot, vecs[pl.ds(at, 1)], 0.0).astype(BF16)
            right = jnp.where(hot, vecs[pl.ds(at + OWNED, 1)], 0.0).astype(BF16)
            base = pl.multiple_of(c * WIDTH, WIDTH)
            q_buf[:, pl.ds(base, HALF)] = left
            q_buf[:, pl.ds(base + HALF, HALF)] = right
            return carry

        lax.fori_loop(0, SLOTS, fill, 0, unroll=True)

    def forward():
        flipped = tiles_t[...].reshape(SLOTS * WIDTH, TILE_ROWS)
        return jnp.dot(q_buf[...], flipped, preferred_element_type=F32)

    def backward():
        def fill(c, carry):
            b = tile_block[0, 0, c]
            picked = rows[pl.ds(tile_row[0, 0, c], 1)]
            base = pl.multiple_of(c * TILE_ROWS, TILE_ROWS)
            p_buf[:, pl.ds(base, TILE_ROWS)] = jnp.where(block_iota == b, picked, 0.0).astype(BF16)
            return carry

        lax.fori_loop(0, SLOTS, fill, 0, unroll=True)
        flat = tiles[...].reshape(SLOTS * TILE_ROWS, WIDTH)
        return jnp.dot(p_buf[...], flat, preferred_element_type=F32)

    def remote(src, dst, send_sem, recv_sem, dev):
        return pltpu.make_async_remote_copy(
            src_ref=src,
            dst_ref=dst,
            send_sem=send_sem,
            recv_sem=recv_sem,
            device_id=dev,
            device_id_type=MESH,
        )

    def send(src, dst, send_sem, recv_sem, dev):
        remote(src, dst, send_sem, recv_sem, dev).start()

    def drain(ref, sem):
        pltpu.make_async_copy(ref, ref, sem).wait()

    def line_start(buf, value, me_at, count, send_sem, recv_sem, dev):
        buf[me_at] = value
        for j in far_first(count, min(count, 8)):
            send(buf.at[me_at], buf.at[me_at], send_sem, recv_sem, dev(j))

    def line_finish(buf, count, send_sem, recv_sem):
        drain(buf.at[pl.ds(0, count - 1)], recv_sem)
        total = buf[0].astype(F32)
        for k in range(1, count):
            total = total + buf[k].astype(F32)
        drain(buf.at[pl.ds(0, count - 1)], send_sem)
        return total

    def flip_tile(c, carry):
        tiles_t[c] = tiles[c].T
        return carry

    sibling = (f, s, 1 - r)
    own_rows = pl.ds(r * SHARE, SHARE)
    hess_copy = remote(
        hess_t.at[own_rows], hess_t.at[own_rows], h_send.at[0], h_recv.at[0], sibling
    )
    thr_copy = remote(thr.at[r], thr.at[r], h_send.at[1], h_recv.at[1], sibling)

    def prepare_hess():
        for copy in later:
            copy.wait()

        def flip_hess(i, carry):
            block = hess[i]
            hess_t[r * SHARE + i] = block.T.astype(BF16)
            on_diag = iota((WIDTH, WIDTH), 0) == iota((WIDTH, WIDTH), 1)
            diagonal = jnp.sum(jnp.where(on_diag, block, 0.0), axis=0, keepdims=True)
            thr[r, pl.ds(i, 1), :] = penalty * diagonal
            return carry

        lax.fori_loop(0, SHARE, flip_hess, 0)
        hess_copy.start()
        thr_copy.start()
        sub = iota((OWNED, WIDTH), 0)

        def find(p, found):
            return found + jnp.where(order[0, p] == s * OWNED + sub, 1, 0)

        first = lax.fori_loop(
            0, BLOCKS // SEGMENTS, find, jnp.zeros((OWNED, WIDTH), jnp.int32), unroll=True
        )
        segment[...] = 1 - first
        most = jnp.zeros((OWNED, WIDTH), jnp.int32)
        for i in range(OWNED):
            most = jnp.where(sub == i, sweeps[s * OWNED + i], most)
        limit[...] = most

    def sum_rows(part, slot, between):
        xb, yb = x_buf.at[slot], y_buf.at[slot]
        xs, xr, ys, yr = x_send.at[slot], x_recv.at[slot], y_send.at[slot], y_recv.at[slot]
        line_start(xb, part.astype(BF16), me_x, NX, xs, xr, x_dev)
        between()
        total = line_finish(xb, NX, xs, xr)
        line_start(yb, total.astype(BF16), me_y, NY, ys, yr, y_dev)
        return line_finish(yb, NY, ys, yr)

    for copy in loads:
        copy.wait()

    for z in range(NZ):
        base = 2 * OWNED * z
        vecs[base : base + OWNED] = weights[pl.ds(base, OWNED, stride=2)]
        vecs[base + OWNED : base + 2 * OWNED] = weights[pl.ds(base + 1, OWNED, stride=2)]
    mine_at = pl.multiple_of(s * 2 * OWNED, 2 * OWNED)
    w_own[:, :HALF] = vecs[pl.ds(mine_at, OWNED)]
    w_own[:, HALF:] = vecs[pl.ds(mine_at + OWNED, OWNED)]
    direc[...] = jnp.zeros((OWNED, WIDTH), F32)
    change_out[...] = jnp.zeros((GROUPS, TILE_ROWS), F32)
    fill_forward()
    for k, copy in enumerate(pieces):
        copy.wait()
        lax.fori_loop(k * per_piece, (k + 1) * per_piece, flip_tile, 0, unroll=True)
    pl.semaphore_wait(barrier, NX + NY + NM - 3)

    def one_round(t, carry):
        def between():
            @pl.when(t == 0)
            def _():
                prepare_hess()

        summed = sum_rows(forward(), t % 2, between)

        @pl.when(t == 0)
        def _():
            prob = jax.nn.sigmoid(summed)
            curv[...] = prob * (1.0 - prob)
            rows[...] = prob - labels[...].astype(F32)

        @pl.when(t > 0)
        def _():
            change = change_out[...] + summed
            change_out[...] = change
            rows[...] = curv[...] * change

        contrib = backward()
        for z in range(NZ):
            block = contrib[OWNED * z : OWNED * (z + 1)]
            rs_out[z] = jnp.concatenate([block[:, :HALF], block[:, HALF:]], axis=0).astype(BF16)
        terms = rs_in.at[t % 2]
        for j in far_first(NM, NZ):
            dev = z_dev(j)
            send(rs_out.at[dev[1]], terms.at[me], z_send.at[0], z_recv.at[t % 2], dev)
        terms[me] = rs_out[s]
        drain(terms.at[pl.ds(0, NM - 1)], z_recv.at[t % 2])
        mine = terms[0].astype(F32)
        for k in range(1, NM):
            mine = mine + terms[k].astype(F32)
        mine = jnp.concatenate([mine[:OWNED], mine[OWNED:]], axis=1)
        drain(terms.at[pl.ds(0, NM - 1)], z_send.at[0])

        @pl.when(t == 0)
        def _():
            grad[...] = mine
            hess_copy.wait()
            thr_copy.wait()

        direction = direc[...]
        model_grad = grad[...] + jnp.where(t > 0, mine, 0.0) + ridge_term * direction
        high = model_grad.astype(BF16).astype(F32)
        pair = jnp.concatenate([high, model_grad - high], axis=0)
        at = iota((2 * OWNED, WIDTH), 0) % OWNED
        parts = [jnp.where(at == i, pair, 0.0).astype(BF16) for i in range(OWNED)]
        product = jnp.dot(
            jnp.concatenate(parts, axis=1),
            hess_t[...].reshape(OWNED * WIDTH, WIDTH),
            preferred_element_type=F32,
        )
        newton = product[:OWNED] + product[OWNED:]
        weight = w_own[...]
        trial = weight + direction - newton
        threshold = jnp.concatenate([thr[0], thr[1]], axis=0)
        size = jnp.maximum(jnp.abs(trial) - threshold, 0.0)
        shrunk = jnp.where(trial > 0.0, size, jnp.where(trial < 0.0, -size, 0.0))
        active = (segment[...] == t % SEGMENTS) & (t // SEGMENTS < limit[...])
        step = jnp.where(active, shrunk - weight - direction, 0.0)
        direc[...] = direction + step

        slot = ag_buf.at[s]
        slot[...] = jnp.concatenate([step[:, :HALF], step[:, HALF:]], axis=0).astype(BF16)
        for j in far_first(NZ, NZ):
            send(slot, slot, z_send.at[1], z_recv.at[2], z_same(j))
        drain(ag_buf.at[pl.ds(0, NZ - 1)], z_recv.at[2])
        vecs[...] = ag_buf[...].reshape(2 * BLOCKS, HALF).astype(F32)
        drain(ag_buf.at[pl.ds(0, NZ - 1)], z_send.at[1])
        fill_forward()
        return carry

    lax.fori_loop(0, ROUNDS, one_round, 0)

    direction = direc[...]
    weight = w_own[...]
    linear = grad[...] * direction + 0.5 * ridge_term * direction * direction
    linear = linear + penalty * (jnp.abs(weight + direction) - jnp.abs(weight))
    linear = jnp.where(iota((OWNED, WIDTH), 0) // SHARE == r, linear, 0.0)
    linear = linear[:, :HALF] + linear[:, HALF:]
    line_start(lx_buf, linear, me_x, NX, l_send.at[0], l_recv.at[0], x_dev)
    part = forward()
    linear = line_finish(lx_buf, NX, l_send.at[0], l_recv.at[0])
    line_start(ly_buf, linear, me_y, NY, l_send.at[1], l_recv.at[1], y_dev)
    summed = sum_rows(part, ROUNDS % 2, lambda: None)
    change = change_out[...] + summed
    linear = line_finish(ly_buf, NY, l_send.at[1], l_recv.at[1])
    quad = 0.5 * curv[...] * change * change
    for g in range(GROUPS // 8):
        linear = linear + quad[8 * g : 8 * g + 8]
    line_start(lz_buf, linear, me, NM, l_send.at[2], l_recv.at[2], z_dev)
    change_out[...] = change
    own = jnp.where(r == 0, direction[:SHARE], direction[SHARE:])
    dir_out[pl.ds(0, SHARE, stride=2)] = own[:, :HALF]
    dir_out[pl.ds(1, SHARE, stride=2)] = own[:, HALF:]
    total = line_finish(lz_buf, NM, l_send.at[2], l_recv.at[2])
    dec_out[...] = jnp.sum(jnp.sum(total, axis=0, keepdims=True), axis=1, keepdims=True)


def on_device(tiles, tile_block, tile_row, labels, weights, hess_inv, order, sweeps):
    vmem = pl.BlockSpec(memory_space=pltpu.VMEM)
    dma = pltpu.SemaphoreType.DMA
    direction, change, decrease = pl.pallas_call(
        body,
        out_shape=(
            jax.ShapeDtypeStruct((8, HALF), F32),
            jax.ShapeDtypeStruct((GROUPS, TILE_ROWS), F32),
            jax.ShapeDtypeStruct((1, 1), F32),
        ),
        in_specs=[pl.BlockSpec(memory_space=pltpu.HBM)] * 8,
        out_specs=[vmem] * 3,
        scratch_shapes=[
            pltpu.SMEM((1, 1, SLOTS), jnp.int32),
            pltpu.SMEM((1, 1, SLOTS), jnp.int32),
            pltpu.SMEM((1, BLOCKS), jnp.int32),
            pltpu.SMEM((BLOCKS,), jnp.int32),
            pltpu.VMEM((SLOTS, TILE_ROWS, WIDTH), BF16),
            pltpu.VMEM((GROUPS, TILE_ROWS), jnp.int32),
            pltpu.VMEM((2 * BLOCKS, HALF), F32),
            pltpu.VMEM((SHARE, WIDTH, WIDTH), F32),
            pltpu.VMEM((SLOTS, WIDTH, TILE_ROWS), BF16),
            pltpu.VMEM((OWNED, WIDTH, WIDTH), BF16),
            pltpu.VMEM((2 * BLOCKS, HALF), F32),
            pltpu.VMEM((GROUPS, TILE_ROWS), F32),
            pltpu.VMEM((GROUPS, SLOTS * WIDTH), BF16),
            pltpu.VMEM((BLOCKS, SLOTS * TILE_ROWS), BF16),
            pltpu.VMEM((2, SHARE, WIDTH), F32),
            pltpu.VMEM((OWNED, WIDTH), F32),
            pltpu.VMEM((OWNED, WIDTH), F32),
            pltpu.VMEM((OWNED, WIDTH), F32),
            pltpu.VMEM((OWNED, WIDTH), jnp.int32),
            pltpu.VMEM((OWNED, WIDTH), jnp.int32),
            pltpu.VMEM((GROUPS, TILE_ROWS), F32),
            pltpu.VMEM((2, NX, GROUPS, TILE_ROWS), BF16),
            pltpu.VMEM((2, NY, GROUPS, TILE_ROWS), BF16),
            pltpu.VMEM((NZ, 2 * OWNED, HALF), BF16),
            pltpu.VMEM((2, NM, 2 * OWNED, HALF), BF16),
            pltpu.VMEM((NZ, 2 * OWNED, HALF), BF16),
            pltpu.VMEM((NX, 8, HALF), F32),
            pltpu.VMEM((NY, 8, HALF), F32),
            pltpu.VMEM((NM, 8, HALF), F32),
            dma((2,)),
            dma((2,)),
            dma((2,)),
            dma((2,)),
            dma((2,)),
            dma((3,)),
            dma((3,)),
            dma((3,)),
            dma((2,)),
            dma((2,)),
            dma((7 + PIECES,)),
        ],
        compiler_params=pltpu.CompilerParams(
            collective_id=0, has_side_effects=True, vmem_limit_bytes=40 * 1024 * 1024
        ),
    )(
        tile_block,
        tile_row,
        order,
        sweeps,
        tiles.reshape(SLOTS, TILE_ROWS, WIDTH),
        labels.reshape(GROUPS, TILE_ROWS),
        weights.reshape(2 * BLOCKS, HALF),
        hess_inv,
    )
    return direction.reshape(-1), change.reshape(-1), decrease.reshape(1)


def solution(mesh):
    in_specs = (
        P("feat", ("samp", "rep"), None, None, None),
        P("feat", ("samp", "rep"), None),
        P("feat", ("samp", "rep"), None),
        P(("samp", "rep")),
        P("feat"),
        P(("feat", "samp", "rep"), None, None),
        P("feat", None),
        P("feat"),
    )
    out_specs = (P(("feat", "samp", "rep")), P(("samp", "rep")), P())
    return jax.shard_map(
        on_device, mesh=mesh, in_specs=in_specs, out_specs=out_specs, check_vma=False
    )
```

time: 156 us -> 156 us (level)
  no operation moved by 1% of the time
where the time goes in v2:
time: 156 us
  Pallas kernels  145 us (93%)
  local copies, waits for them, and re-layouts  8.18 us (5%)
  between operations  2.47 us (2%)
    pallas_call x1, Pallas kernels, on_device(): pl.pallas_call(body, out_shape=(jax.ShapeDtypeStruct((8, HALF), F32), jax...  145 us
    unnamed x18, local copies, waits for them, and re-layouts  8.18 us

profile of v2, /device:TPU:1, one launch (start us, length us, event | category | flops | bytes accessed | tf_op | source)
XLA Modules:
  0.0 155.6 jit_solution(9276139649009421260)
XLA Ops:
  0.6 0.0 copy-start
  0.6 1.6 %copy-done = bf16[1,1,32,128,256]{4,3,2,1,0:T(8,128)(2,1)S(1)} copy-done((bf16[1,1,32,128,256]{4,3,2,1,0:T(8,128)(2,1)S(1)}, bf16[1,1,32,128,256]{4,3,2,1,0:T(8,128)(2,1)}, u32[]{:S(2)}) %copy-start) | copy-done | bytes 2097176
  2.2 0.0 copy-start.1
  2.2 1.2 copy-done.1
  3.5 0.0 copy-start.2
  3.5 0.8 copy-done.2
  4.3 0.0 copy-start.3
  4.3 0.7 copy-done.3
  5.0 0.0 copy-start.4
  5.0 0.7 copy-done.4
  5.7 0.0 copy-start.5
  5.7 0.7 copy-done.5
  6.3 0.0 copy-start.6
  6.3 0.7 copy-done.6
  7.0 0.0 copy-start.7
  7.0 0.7 copy-done.7
  7.6 144.9 %shard_map.103 = (f32[8,128]{1,0:T(8,128)S(1)}, f32[32,128]{1,0:T(8,128)S(1)}, f32[1,1]{1,0:T(1,128)}) custom-call(s32[1,1,32]{2,1,0:T(1,128)S(1)} %copy-done.4, s32[1,1,32]{2,1,0:T(1,128)S(1)} %copy-done.5, s32[1,64]{1,0:T(1,128)S(1)} %copy-done.6, s32[64]{0:T(128)S(1)} %copy-done.7, bf16[32,128,256]{2,1,0:T(8,128)(2,1)S(1)} %bitcast.6, ...), custom_call_target="tpu_custom_call" | custom-call | tf_op jit(solution)/shard_map/pallas_call | solution.py:380
  152.5 0.6 copy.14
  153.1 0.6 copy.15
Async XLA Ops:
  0.6 1.6 %copy-start = (bf16[1,1,32,128,256]{4,3,2,1,0:T(8,128)(2,1)S(1)}, bf16[1,1,32,128,256]{4,3,2,1,0:T(8,128)(2,1)}, u32[]{:S(2)}) copy-start(bf16[1,1,32,128,256]{4,3,2,1,0:T(8,128)(2,1)} %param.8) | copy-start | bytes 6291460
  2.2 1.2 copy-start.1
  3.5 0.8 copy-start.2
  4.3 0.7 copy-start.3
  5.0 0.7 copy-start.4
  5.7 0.7 copy-start.5
  6.3 0.7 copy-start.6
  7.0 0.7 copy-start.7

commit v3 on v2

--- a/solution.py
+++ b/solution.py
@@ -111,6 +111,11 @@
     def z_same(j):
         return (f, (s + j) % NZ, r)
 
+    barrier = pltpu.get_barrier_semaphore()
+    for dev, count in ((y_dev, NY), (z_dev, NM), (x_dev, NX)):
+        for j in far_first(count, min(count, 8)):
+            pl.semaphore_signal(barrier, inc=1, device_id=dev(j), device_id_type=MESH)
+
     def load(src, dst, k):
         return pltpu.make_async_copy(src, dst, load_sem.at[k])
 
@@ -137,11 +142,6 @@
     for copy in loads + pieces + later:
         copy.start()
 
-    barrier = pltpu.get_barrier_semaphore()
-    for dev, count in ((x_dev, NX), (y_dev, NY), (z_dev, NM)):
-        for j in range(1, count):
-            pl.semaphore_signal(barrier, inc=1, device_id=dev(j), device_id_type=MESH)
-
     row_iota = iota((GROUPS, HALF), 0)
     block_iota = iota((BLOCKS, TILE_ROWS), 0)
 
@@ -355,12 +355,16 @@
     linear = linear + penalty * (jnp.abs(weight + direction) - jnp.abs(weight))
     linear = jnp.where(iota((OWNED, WIDTH), 0) // SHARE == r, linear, 0.0)
     linear = linear[:, :HALF] + linear[:, HALF:]
+    slot = ROUNDS % 2
+    xb, yb = x_buf.at[slot], y_buf.at[slot]
+    xs, xr, ys, yr = x_send.at[slot], x_recv.at[slot], y_send.at[slot], y_recv.at[slot]
+    line_start(xb, forward().astype(BF16), me_x, NX, xs, xr, x_dev)
     line_start(lx_buf, linear, me_x, NX, l_send.at[0], l_recv.at[0], x_dev)
-    part = forward()
+    total = line_finish(xb, NX, xs, xr)
+    line_start(yb, total.astype(BF16), me_y, NY, ys, yr, y_dev)
     linear = line_finish(lx_buf, NX, l_send.at[0], l_recv.at[0])
     line_start(ly_buf, linear, me_y, NY, l_send.at[1], l_recv.at[1], y_dev)
-    summed = sum_rows(part, ROUNDS % 2, lambda: None)
-    change = change_out[...] + summed
+    change = change_out[...] + line_finish(yb, NY, ys, yr)
     linear = line_finish(ly_buf, NY, l_send.at[1], l_recv.at[1])
     quad = 0.5 * curv[...] * change * change
     for g in range(GROUPS // 8):
@@ -429,7 +433,7 @@
             dma((7 + PIECES,)),
         ],
         compiler_params=pltpu.CompilerParams(
-            collective_id=0, has_side_effects=True, vmem_limit_bytes=40 * 1024 * 1024
+            collective_id=0, has_side_effects=True, vmem_limit_bytes=60 * 1024 * 1024
         ),
     )(
         tile_block,

time: 156 us -> 148 us (0.949)
  local copies, waits for them, and re-layouts: 8.18 us -> 2.59 us
  Pallas kernels: 145 us -> 142 us
    unnamed x18 -> x2, local copies, waits for them, and re-layouts: 8.18 us -> 2.59 us
    pallas_call x1, Pallas kernels: 145 us -> 142 us  [on_device(): pl.pallas_call(body, out_shape=(jax.ShapeDtypeStruct((8, HALF), F32), jax...]
where the time goes in v3:
time: 148 us; the launch traced here: 147 us
  Pallas kernels  142 us (96%)
  local copies, waits for them, and re-layouts  2.59 us (2%)
  between operations  2.4 us (2%)
    pallas_call x1, Pallas kernels, on_device(): pl.pallas_call(body, out_shape=(jax.ShapeDtypeStruct((8, HALF), F32), jax...  142 us

profile of v3, /device:TPU:1, one launch (start us, length us, event | category | flops | bytes accessed | tf_op | source)
XLA Modules:
  0.0 147.3 jit_solution(16571834272472208054)
XLA Ops:
  0.6 142.3 %shard_map.103 = (f32[8,128]{1,0:T(8,128)}, f32[32,128]{1,0:T(8,128)}, f32[1,1]{1,0:T(1,128)}) custom-call(s32[1,1,32]{2,1,0:T(1,128)} %tile_block_hbm.1, s32[1,1,32]{2,1,0:T(1,128)} %tile_row_hbm.1, s32[1,64]{1,0:T(1,128)} %order_hbm.1, s32[64]{0:T(128)} %sweeps_hbm.1, bf16[32,128,256]{2,1,0:T(8,128)(2,1)} %bitcast.6, s32[32,128]{1,0:T(8,128)} %bitcast.8, ...), custom_call_target="tpu_custom_call" | custom-call | tf_op jit(solution)/shard_map/pallas_call | solution.py:384
  142.9 1.3 copy.14
  144.2 1.3 copy.15

commit v4 on v3

--- a/solution.py
+++ b/solution.py
@@ -35,7 +35,7 @@
 
 def far_first(count, chips):
     per = count // chips
-    return sorted(range(1, count), key=lambda j: -min(j // per, chips - j // per))
+    return sorted(range(1, count), key=lambda j: (-min(j // per, chips - j // per), -(j % per)))
 
 
 def iota(shape, dim):
@@ -176,7 +176,9 @@
 
         lax.fori_loop(0, SLOTS, fill, 0, unroll=True)
         flat = tiles[...].reshape(SLOTS * TILE_ROWS, WIDTH)
-        return jnp.dot(p_buf[...], flat, preferred_element_type=F32)
+        left = jnp.dot(p_buf[...], flat[:, :HALF], preferred_element_type=F32)
+        right = jnp.dot(p_buf[...], flat[:, HALF:], preferred_element_type=F32)
+        return left, right
 
     def remote(src, dst, send_sem, recv_sem, dev):
         return pltpu.make_async_remote_copy(
@@ -294,10 +296,10 @@
             change_out[...] = change
             rows[...] = curv[...] * change
 
-        contrib = backward()
+        left, right = backward()
         for z in range(NZ):
-            block = contrib[OWNED * z : OWNED * (z + 1)]
-            rs_out[z] = jnp.concatenate([block[:, :HALF], block[:, HALF:]], axis=0).astype(BF16)
+            at = slice(OWNED * z, OWNED * (z + 1))
+            rs_out[z] = jnp.concatenate([left[at], right[at]], axis=0).astype(BF16)
         terms = rs_in.at[t % 2]
         for j in far_first(NM, NZ):
             dev = z_dev(j)
@@ -378,8 +380,18 @@
     dec_out[...] = jnp.sum(jnp.sum(total, axis=0, keepdims=True), axis=1, keepdims=True)
 
 
+def write_out(direction, change, dir_out, change_out, sem):
+    first = pltpu.make_async_copy(direction, dir_out, sem.at[0])
+    second = pltpu.make_async_copy(change, change_out, sem.at[1])
+    first.start()
+    second.start()
+    first.wait()
+    second.wait()
+
+
 def on_device(tiles, tile_block, tile_row, labels, weights, hess_inv, order, sweeps):
     vmem = pl.BlockSpec(memory_space=pltpu.VMEM)
+    hbm = pl.BlockSpec(memory_space=pltpu.HBM)
     dma = pltpu.SemaphoreType.DMA
     direction, change, decrease = pl.pallas_call(
         body,
@@ -388,7 +400,7 @@
             jax.ShapeDtypeStruct((GROUPS, TILE_ROWS), F32),
             jax.ShapeDtypeStruct((1, 1), F32),
         ),
-        in_specs=[pl.BlockSpec(memory_space=pltpu.HBM)] * 8,
+        in_specs=[hbm] * 8,
         out_specs=[vmem] * 3,
         scratch_shapes=[
             pltpu.SMEM((1, 1, SLOTS), jnp.int32),
@@ -445,6 +457,17 @@
         weights.reshape(2 * BLOCKS, HALF),
         hess_inv,
     )
+    direction, change = pl.pallas_call(
+        write_out,
+        out_shape=(
+            jax.ShapeDtypeStruct((8, HALF), F32),
+            jax.ShapeDtypeStruct((GROUPS, TILE_ROWS), F32),
+        ),
+        in_specs=[hbm] * 2,
+        out_specs=[hbm] * 2,
+        scratch_shapes=[dma((2,))],
+        compiler_params=pltpu.CompilerParams(vmem_limit_bytes=60 * 1024 * 1024),
+    )(direction, change)
     return direction.reshape(-1), change.reshape(-1), decrease.reshape(1)
 
 

time: 148 us -> 146 us (0.986)
  local copies, waits for them, and re-layouts: 2.59 us -> 0 us
    unnamed x2 -> x0, local copies, waits for them, and re-layouts: 2.59 us -> none
    pallas_call x0 -> x1, Pallas kernels: none -> 1.74 us  [on_device(): pl.pallas_call(write_out, out_shape=(jax.ShapeDtypeStruct((8, HALF), F32)...]
where the time goes in v4:
time: 146 us
  Pallas kernels  143 us (98%)
  between operations  2.38 us (2%)
    pallas_call x1, Pallas kernels, on_device(): pl.pallas_call(body, out_shape=(jax.ShapeDtypeStruct((8, HALF), F32), jax...  142 us

profile of v4, /device:TPU:1, one launch (start us, length us, event | category | flops | bytes accessed | tf_op | source)
XLA Modules:
  0.0 145.6 jit_solution(5074301814749033927)
XLA Ops:
  0.6 141.5 %shard_map.103 = (f32[8,128]{1,0:T(8,128)}, f32[32,128]{1,0:T(8,128)}, f32[1,1]{1,0:T(1,128)}) custom-call(s32[1,1,32]{2,1,0:T(1,128)} %tile_block_hbm.1, s32[1,1,32]{2,1,0:T(1,128)} %tile_row_hbm.1, s32[1,64]{1,0:T(1,128)} %order_hbm.1, s32[64]{0:T(128)} %sweeps_hbm.1, bf16[32,128,256]{2,1,0:T(8,128)(2,1)} %bitcast.6, s32[32,128]{1,0:T(8,128)} %bitcast.8, ...), custom_call_target="tpu_custom_call" | custom-call | tf_op jit(solution)/shard_map/pallas_call | solution.py:396
  142.2 1.7 %shard_map.104 = (f32[8,128]{1,0:T(8,128)}, f32[32,128]{1,0:T(8,128)}) custom-call(f32[8,128]{1,0:T(8,128)} %get-tuple-element.8.direction, f32[32,128]{1,0:T(8,128)} %get-tuple-element.9.change), custom_call_target="tpu_custom_call" | custom-call | tf_op jit(solution)/shard_map/pallas_call | solution.py:460

commit v5 on v4

--- a/solution.py
+++ b/solution.py
@@ -277,22 +277,14 @@
     pl.semaphore_wait(barrier, NX + NY + NM - 3)
 
     def one_round(t, carry):
-        def between():
-            @pl.when(t == 0)
-            def _():
-                prepare_hess()
-
-        summed = sum_rows(forward(), t % 2, between)
-
-        @pl.when(t == 0)
-        def _():
+        opening = isinstance(t, int)
+        if opening:
+            summed = sum_rows(forward(), t % 2, prepare_hess)
             prob = jax.nn.sigmoid(summed)
             curv[...] = prob * (1.0 - prob)
             rows[...] = prob - labels[...].astype(F32)
-
-        @pl.when(t > 0)
-        def _():
-            change = change_out[...] + summed
+        else:
+            change = change_out[...] + sum_rows(forward(), t % 2, lambda: None)
             change_out[...] = change
             rows[...] = curv[...] * change
 
@@ -312,22 +304,26 @@
         mine = jnp.concatenate([mine[:OWNED], mine[OWNED:]], axis=1)
         drain(terms.at[pl.ds(0, NM - 1)], z_send.at[0])
 
-        @pl.when(t == 0)
-        def _():
+        direction = direc[...]
+        if opening:
             grad[...] = mine
             hess_copy.wait()
             thr_copy.wait()
-
-        direction = direc[...]
-        model_grad = grad[...] + jnp.where(t > 0, mine, 0.0) + ridge_term * direction
+            model_grad = mine
+        else:
+            model_grad = grad[...] + mine + ridge_term * direction
         high = model_grad.astype(BF16).astype(F32)
         pair = jnp.concatenate([high, model_grad - high], axis=0)
         at = iota((2 * OWNED, WIDTH), 0) % OWNED
         parts = [jnp.where(at == i, pair, 0.0).astype(BF16) for i in range(OWNED)]
-        product = jnp.dot(
-            jnp.concatenate(parts, axis=1),
-            hess_t[...].reshape(OWNED * WIDTH, WIDTH),
-            preferred_element_type=F32,
+        spread = jnp.concatenate(parts, axis=1)
+        flipped = hess_t[...].reshape(OWNED * WIDTH, WIDTH)
+        product = jnp.concatenate(
+            [
+                jnp.dot(spread, flipped[:, :HALF], preferred_element_type=F32),
+                jnp.dot(spread, flipped[:, HALF:], preferred_element_type=F32),
+            ],
+            axis=1,
         )
         newton = product[:OWNED] + product[OWNED:]
         weight = w_own[...]
@@ -349,7 +345,8 @@
         fill_forward()
         return carry
 
-    lax.fori_loop(0, ROUNDS, one_round, 0)
+    one_round(0, 0)
+    lax.fori_loop(1, ROUNDS, one_round, 0)
 
     direction = direc[...]
     weight = w_own[...]
@@ -380,13 +377,9 @@
     dec_out[...] = jnp.sum(jnp.sum(total, axis=0, keepdims=True), axis=1, keepdims=True)
 
 
-def write_out(direction, change, dir_out, change_out, sem):
-    first = pltpu.make_async_copy(direction, dir_out, sem.at[0])
-    second = pltpu.make_async_copy(change, change_out, sem.at[1])
-    first.start()
-    second.start()
-    first.wait()
-    second.wait()
+def write_out(direction, change, dir_out, change_out):
+    dir_out[...] = direction[...]
+    change_out[...] = change[...]
 
 
 def on_device(tiles, tile_block, tile_row, labels, weights, hess_inv, order, sweeps):
@@ -463,9 +456,8 @@
             jax.ShapeDtypeStruct((8, HALF), F32),
             jax.ShapeDtypeStruct((GROUPS, TILE_ROWS), F32),
         ),
-        in_specs=[hbm] * 2,
-        out_specs=[hbm] * 2,
-        scratch_shapes=[dma((2,))],
+        in_specs=[vmem] * 2,
+        out_specs=[vmem] * 2,
         compiler_params=pltpu.CompilerParams(vmem_limit_bytes=60 * 1024 * 1024),
     )(direction, change)
     return direction.reshape(-1), change.reshape(-1), decrease.reshape(1)

time: 146 us -> 146 us (level)
  no operation moved by 1% of the time
where the time goes in v5:
time: 146 us
  Pallas kernels  143 us (98%)
  between operations  2.38 us (2%)
    pallas_call x1, Pallas kernels, on_device(): pl.pallas_call(body, out_shape=(jax.ShapeDtypeStruct((8, HALF), F32), jax...  142 us

profile of v5, /device:TPU:1, one launch (start us, length us, event | category | flops | bytes accessed | tf_op | source)
XLA Modules:
  0.0 145.7 jit_solution(16228285608096607776)
XLA Ops:
  0.6 141.9 %shard_map.103 = (f32[8,128]{1,0:T(8,128)}, f32[32,128]{1,0:T(8,128)}, f32[1,1]{1,0:T(1,128)}) custom-call(s32[1,1,32]{2,1,0:T(1,128)} %tile_block_hbm.1, s32[1,1,32]{2,1,0:T(1,128)} %tile_row_hbm.1, s32[1,64]{1,0:T(1,128)} %order_hbm.1, s32[64]{0:T(128)} %sweeps_hbm.1, bf16[32,128,256]{2,1,0:T(8,128)(2,1)} %bitcast.6, s32[32,128]{1,0:T(8,128)} %bitcast.8, ...), custom_call_target="tpu_custom_call" | custom-call | tf_op jit(solution)/shard_map/pallas_call | solution.py:389
  142.6 1.3 shard_map.104

commit v6 on v5

--- a/solution.py
+++ b/solution.py
@@ -24,6 +24,22 @@
 OWNED = 8
 SHARE = 4
 PIECES = 4
+
+SIDE = ((1, 0), (3, 0))
+ARM = ((0, 3), (0, 5), (0, 2), (0, 6), (0, 1), (0, 7))
+FAR = (
+    (2, 4),
+    (1, 4),
+    (3, 4),
+    (2, 3),
+    (2, 5),
+    (2, 2),
+    (2, 6),
+    (0, 4),
+    (2, 1),
+    (2, 7),
+    (2, 0),
+)
 
 penalty = 0.05
 ridge_term = 0.1
@@ -77,6 +93,10 @@
     curv,
     x_buf,
     y_buf,
+    parts_sum,
+    side_buf,
+    arm_buf,
+    far_buf,
     rs_out,
     rs_in,
     ag_buf,
@@ -87,6 +107,8 @@
     x_recv,
     y_send,
     y_recv,
+    n_send,
+    n_recv,
     z_send,
     z_recv,
     l_send,
@@ -111,7 +133,13 @@
     def z_same(j):
         return (f, (s + j) % NZ, r)
 
+    def plane_dev(dx, dy):
+        return ((me_y + dy) % NY * NX + (me_x + dx) % NX, s, r)
+
     barrier = pltpu.get_barrier_semaphore()
+    for dx, dy in FAR:
+        if dx and dy:
+            pl.semaphore_signal(barrier, inc=1, device_id=plane_dev(dx, dy), device_id_type=MESH)
     for dev, count in ((y_dev, NY), (z_dev, NM), (x_dev, NX)):
         for j in far_first(count, min(count, 8)):
             pl.semaphore_signal(barrier, inc=1, device_id=dev(j), device_id_type=MESH)
@@ -258,6 +286,33 @@
         line_start(yb, total.astype(BF16), me_y, NY, ys, yr, y_dev)
         return line_finish(yb, NY, ys, yr)
 
+    def near_sum(part, slot):
+        side, arm, far = side_buf.at[slot], arm_buf.at[slot], far_buf.at[slot]
+        stages = ((side, SIDE, 0), (arm, ARM, 1), (far, FAR, 2))
+
+        def start(stage, value):
+            buf, offsets, k = stage
+            last = len(offsets)
+            buf[last] = value.astype(BF16)
+            for j, (dx, dy) in enumerate(offsets):
+                send(buf.at[last], buf.at[j], n_send.at[slot, k], n_recv.at[slot, k], plane_dev(dx, dy))
+
+        def finish(stage, total):
+            buf, offsets, k = stage
+            got = buf.at[pl.ds(0, len(offsets))]
+            drain(got, n_recv.at[slot, k])
+            for j in range(len(offsets)):
+                total = total + buf[j].astype(F32)
+            drain(got, n_send.at[slot, k])
+            return total
+
+        start(stages[0], part)
+        start(stages[2], part)
+        triple = finish(stages[0], part)
+        start(stages[1], triple)
+        total = finish(stages[2], triple)
+        return finish(stages[1], total)
+
     for copy in loads:
         copy.wait()
 
@@ -270,11 +325,12 @@
     w_own[:, HALF:] = vecs[pl.ds(mine_at + OWNED, OWNED)]
     direc[...] = jnp.zeros((OWNED, WIDTH), F32)
     change_out[...] = jnp.zeros((GROUPS, TILE_ROWS), F32)
+    parts_sum[...] = jnp.zeros((GROUPS, TILE_ROWS), F32)
     fill_forward()
     for k, copy in enumerate(pieces):
         copy.wait()
         lax.fori_loop(k * per_piece, (k + 1) * per_piece, flip_tile, 0, unroll=True)
-    pl.semaphore_wait(barrier, NX + NY + NM - 3)
+    pl.semaphore_wait(barrier, NX + NY + NM - 3 + sum(1 for dx, dy in FAR if dx and dy))
 
     def one_round(t, carry):
         opening = isinstance(t, int)
@@ -284,7 +340,9 @@
             curv[...] = prob * (1.0 - prob)
             rows[...] = prob - labels[...].astype(F32)
         else:
-            change = change_out[...] + sum_rows(forward(), t % 2, lambda: None)
+            part = forward()
+            parts_sum[...] += part
+            change = change_out[...] + near_sum(part, t % 2)
             change_out[...] = change
             rows[...] = curv[...] * change
 
@@ -354,16 +412,16 @@
     linear = linear + penalty * (jnp.abs(weight + direction) - jnp.abs(weight))
     linear = jnp.where(iota((OWNED, WIDTH), 0) // SHARE == r, linear, 0.0)
     linear = linear[:, :HALF] + linear[:, HALF:]
-    slot = ROUNDS % 2
+    slot = 1
     xb, yb = x_buf.at[slot], y_buf.at[slot]
     xs, xr, ys, yr = x_send.at[slot], x_recv.at[slot], y_send.at[slot], y_recv.at[slot]
-    line_start(xb, forward().astype(BF16), me_x, NX, xs, xr, x_dev)
+    line_start(xb, (parts_sum[...] + forward()).astype(BF16), me_x, NX, xs, xr, x_dev)
     line_start(lx_buf, linear, me_x, NX, l_send.at[0], l_recv.at[0], x_dev)
     total = line_finish(xb, NX, xs, xr)
     line_start(yb, total.astype(BF16), me_y, NY, ys, yr, y_dev)
     linear = line_finish(lx_buf, NX, l_send.at[0], l_recv.at[0])
     line_start(ly_buf, linear, me_y, NY, l_send.at[1], l_recv.at[1], y_dev)
-    change = change_out[...] + line_finish(yb, NY, ys, yr)
+    change = line_finish(yb, NY, ys, yr)
     linear = line_finish(ly_buf, NY, l_send.at[1], l_recv.at[1])
     quad = 0.5 * curv[...] * change * change
     for g in range(GROUPS // 8):
@@ -419,6 +477,10 @@
             pltpu.VMEM((GROUPS, TILE_ROWS), F32),
             pltpu.VMEM((2, NX, GROUPS, TILE_ROWS), BF16),
             pltpu.VMEM((2, NY, GROUPS, TILE_ROWS), BF16),
+            pltpu.VMEM((GROUPS, TILE_ROWS), F32),
+            pltpu.VMEM((2, len(SIDE) + 1, GROUPS, TILE_ROWS), BF16),
+            pltpu.VMEM((2, len(ARM) + 1, GROUPS, TILE_ROWS), BF16),
+            pltpu.VMEM((2, len(FAR) + 1, GROUPS, TILE_ROWS), BF16),
             pltpu.VMEM((NZ, 2 * OWNED, HALF), BF16),
             pltpu.VMEM((2, NM, 2 * OWNED, HALF), BF16),
             pltpu.VMEM((NZ, 2 * OWNED, HALF), BF16),
@@ -429,6 +491,8 @@
             dma((2,)),
             dma((2,)),
             dma((2,)),
+            dma((2, 3)),
+            dma((2, 3)),
             dma((2,)),
             dma((3,)),
             dma((3,)),

time: 146 us -> 144 us (0.986)
  Pallas kernels: 143 us -> 141 us
    pallas_call x1, Pallas kernels: 142 us -> 140 us  [on_device(): pl.pallas_call(body, out_shape=(jax.ShapeDtypeStruct((8, HALF), F32), jax...]
where the time goes in v6:
time: 144 us; the launch traced here: 143 us
  Pallas kernels  141 us (98%)
  between operations  2.38 us (2%)
    pallas_call x1, Pallas kernels, on_device(): pl.pallas_call(body, out_shape=(jax.ShapeDtypeStruct((8, HALF), F32), jax...  140 us

profile of v6, /device:TPU:1, one launch (start us, length us, event | category | flops | bytes accessed | tf_op | source)
XLA Modules:
  0.0 143.3 jit_solution(1925571673780432689)
XLA Ops:
  0.6 139.6 %shard_map.103 = (f32[8,128]{1,0:T(8,128)}, f32[32,128]{1,0:T(8,128)}, f32[1,1]{1,0:T(1,128)}) custom-call(s32[1,1,32]{2,1,0:T(1,128)} %tile_block_hbm.1, s32[1,1,32]{2,1,0:T(1,128)} %tile_row_hbm.1, s32[1,64]{1,0:T(1,128)} %order_hbm.1, s32[64]{0:T(128)} %sweeps_hbm.1, bf16[32,128,256]{2,1,0:T(8,128)(2,1)} %bitcast.6, s32[32,128]{1,0:T(8,128)} %bitcast.8, ...), custom_call_target="tpu_custom_call" | custom-call | tf_op jit(solution)/shard_map/pallas_call | solution.py:447
  140.2 1.3 shard_map.104

commit v7 on v6

--- a/solution.py
+++ b/solution.py
@@ -333,7 +333,7 @@
     pl.semaphore_wait(barrier, NX + NY + NM - 3 + sum(1 for dx, dy in FAR if dx and dy))
 
     def one_round(t, carry):
-        opening = isinstance(t, int)
+        opening = t == 0
         if opening:
             summed = sum_rows(forward(), t % 2, prepare_hess)
             prob = jax.nn.sigmoid(summed)
@@ -403,8 +403,8 @@
         fill_forward()
         return carry
 
-    one_round(0, 0)
-    lax.fori_loop(1, ROUNDS, one_round, 0)
+    for t in range(ROUNDS):
+        one_round(t, 0)
 
     direction = direc[...]
     weight = w_own[...]

time: 144 us -> 143 us (level)
  no operation moved by 1% of the time
where the time goes in v7:
time: 143 us
  Pallas kernels  141 us (99%)
  between operations  2.38 us (2%)
    pallas_call x1, Pallas kernels, on_device(): pl.pallas_call(body, out_shape=(jax.ShapeDtypeStruct((8, HALF), F32), jax...  139 us

profile of v7, /device:TPU:1, one launch (start us, length us, event | category | flops | bytes accessed | tf_op | source)
XLA Modules:
  0.0 143.2 jit_solution(5071504694420400576)
XLA Ops:
  0.6 139.4 %shard_map.103 = (f32[8,128]{1,0:T(8,128)}, f32[32,128]{1,0:T(8,128)}, f32[1,1]{1,0:T(1,128)}) custom-call(s32[1,1,32]{2,1,0:T(1,128)} %tile_block_hbm.1, s32[1,1,32]{2,1,0:T(1,128)} %tile_row_hbm.1, s32[1,64]{1,0:T(1,128)} %order_hbm.1, s32[64]{0:T(128)} %sweeps_hbm.1, bf16[32,128,256]{2,1,0:T(8,128)(2,1)} %bitcast.6, s32[32,128]{1,0:T(8,128)} %bitcast.8, ...), custom_call_target="tpu_custom_call" | custom-call | tf_op jit(solution)/shard_map/pallas_call | solution.py:447
  140.1 1.3 shard_map.104
